TPU v7x, 512 devices: a whole 4x8x8 slice. The times are simulated.
512 devices in a mesh: sec: 64 (over x, z, core), term: 8 (over y).
Axes of the slice: x: 4, y: 8, z: 8, core: 2. Of those that a mesh axis runs over, the one named last changes fastest.
Arguments:
- wavefunction: bfloat16 [3, 16384, 256], P(None, 'sec'), may hold values from -6 to 6
- left_blocks: bfloat16 [128, 64, 256, 256], P('term', 'sec'), may hold values from -0.03125 to 0.03125
- right_blocks: bfloat16 [128, 64, 256, 256], P('term', 'sec'), may hold values from -0.375 to 0.375
- term_shift: int32 [128], P('term'), may hold values from -2 to 2, as said below
- left_sizes: int32 [64], replicated, may hold values from 64 to 256, as said below
- right_sizes: int32 [64], replicated, may hold values from 64 to 256, as said below
Outputs:
- sigma: bfloat16 [3, 16384, 256], P(None, ('sec', 'term'))
Inputs may be any that keep to these rules, and one draw needn't show every extreme that they name: `term_shift`: every offset from -2 to 2 is taken by some term. `left_sizes`: valid states of each left sector; rows beyond them in its 256 are padding; some sector has all 256. `right_sizes`: valid states of each right sector; columns beyond them in its 256 are padding; some sector has all 256.
All inputs are finite; a program needn't handle non-finite values.
Results may differ from a plain program's by a relative error of at most 0.0049.
Values may be sent and summed in bfloat16 or wider, within the bound.
A program may use at most 64 MiB of HBM per device.

v0:
```python
import jax
import jax.numpy as jnp
from jax import lax
from jax.sharding import PartitionSpec as P


def from_behind(value, axis, by):
    count = lax.axis_size(axis)
    pairs = [(i, i + by) for i in range(count) if 0 <= i + by < count]
    return lax.ppermute(value, axis, pairs)


def per_device(wavefunction, left_blocks, right_blocks, term_shift, left_sizes, right_sizes):
    block_rows = wavefunction.shape[1]
    col_count = wavefunction.shape[2]
    sector_index = lax.axis_index("sec")
    own_rows = lax.dynamic_index_in_dim(left_sizes, sector_index, keepdims=False)
    own_cols = lax.dynamic_index_in_dim(right_sizes, sector_index, keepdims=False)
    row_ok = jnp.arange(block_rows) < own_rows
    col_ok = jnp.arange(col_count) < own_cols
    valid_own = (row_ok[:, None] & col_ok[None, :]).astype(jnp.bfloat16)
    masked = wavefunction * valid_own[None]
    arrived = []
    for offset in (2, 1, -1, -2):
        arrived.append(from_behind(masked, "sec", offset))
    sources = jnp.stack([arrived[0], arrived[1], masked, arrived[2], arrived[3]])
    selected = jnp.take(sources, term_shift + 2, axis=0)
    products = jnp.einsum(
        "kab,kvbc->kvac", left_blocks[:, 0], selected, preferred_element_type=jnp.float32
    ).astype(jnp.bfloat16)
    partial_value = jnp.einsum(
        "kvac,kdc->vad", products, right_blocks[:, 0], preferred_element_type=jnp.float32
    )
    summed = lax.psum_scatter(partial_value, "term", scatter_dimension=1, tiled=True)
    row_piece = block_rows // lax.axis_size("term")
    row_mine = lax.dynamic_slice_in_dim(row_ok, lax.axis_index("term") * row_piece, row_piece)
    valid_mine = (row_mine[:, None] & col_ok[None, :]).astype(jnp.float32)
    return (summed * valid_mine[None]).astype(jnp.bfloat16)


def solution(mesh):
    placed = (
        P(None, "sec", None),
        P("term", "sec", None, None),
        P("term", "sec", None, None),
        P("term"),
        P(),
        P(),
    )
    return jax.shard_map(
        per_device,
        mesh=mesh,
        in_specs=placed,
        out_specs=P(None, ("sec", "term"), None),
        check_vma=False,
    )
```

profile of v0, /device:TPU:2, one launch (start us, length us, event | category | flops | bytes accessed | tf_op | source)
XLA Modules:
  0.0 103.8 jit_solution(4190678141664979469)
XLA Ops:
  6.5 0.0 copy-start
  6.5 0.0 copy-start.1
  6.5 0.0 reduce-scatter.2.cloned.1.call-start
  6.5 1.5 %dynamic_slice.10 = s32[1]{0:T(128)} dynamic-slice(s32[64]{0:T(128)} %param.10, s32[]{:T(128)S(6)} %select_n.18), dynamic_slice_sizes={1} | dynamic-slice | bytes 12 | tf_op jit(solution)/shard_map/jit(dynamic_index_in_dim)/dynamic_slice | solution.py:17
  8.0 1.2 %dynamic_slice.11 = s32[1]{0:T(128)} dynamic-slice(s32[64]{0:T(128)} %param.11, s32[]{:T(128)S(6)} %select_n.18), dynamic_slice_sizes={1} | dynamic-slice | bytes 12 | tf_op jit(solution)/shard_map/jit(dynamic_index_in_dim)/dynamic_slice | solution.py:18
  9.2 1.3 %iota_compare_fusion = (pred[256]{0:T(512)(128)(4,1)S(1)}, pred[256]{0:T(512)(128)(4,1)S(1)}) fusion(s32[]{:T(128)} %bitcast.1, s32[]{:T(128)} %bitcast), kind=kLoop, calls=%fused_computation.22 | loop fusion | flops 512 | bytes 520 | tf_op jit(solution)/shard_map/lt | solution.py:20
  10.6 0.1 and_convert_fusion
  10.7 1.0 broadcast_multiply_fusion
  11.7 4.3 %collective-permute-start = (bf16[3,256,256]{2,1,0:T(8,128)(2,1)S(1)}, bf16[3,256,256]{2,1,0:T(8,128)(2,1)S(1)}, u32[]{:S(2)}, u32[]{:S(2)}) collective-permute-start(bf16[3,256,256]{2,1,0:T(8,128)(2,1)S(1)} %broadcast_multiply_fusion), channel_id=1, source_target_pairs={{0,16},{8,24},{16,32},{24,40},{32,48},{40,56},{48,64},{56,72},{64,... | collective-permute-start | bytes 1179656 | tf_op jit(solution)/shard_map/ppermute | solution.py:10
  16.0 1.9 %collective-permute-start.1 = (bf16[3,256,256]{2,1,0:T(8,128)(2,1)S(1)}, bf16[3,256,256]{2,1,0:T(8,128)(2,1)S(1)}, u32[]{:S(2)}, u32[]{:S(2)}) collective-permute-start(bf16[3,256,256]{2,1,0:T(8,128)(2,1)S(1)} %broadcast_multiply_fusion), channel_id=1, source_target_pairs={{0,8},{8,16},{16,24},{24,32},{32,40},{40,48},{48,56},{56,64},{64,7... | collective-permute-start | bytes 1179656 | tf_op jit(solution)/shard_map/ppermute | solution.py:10
  17.9 8.0 %collective-permute-start.2 = (bf16[3,256,256]{2,1,0:T(8,128)(2,1)S(1)}, bf16[3,256,256]{2,1,0:T(8,128)(2,1)S(1)}, u32[]{:S(2)}, u32[]{:S(2)}) collective-permute-start(bf16[3,256,256]{2,1,0:T(8,128)(2,1)S(1)} %broadcast_multiply_fusion), channel_id=1, source_target_pairs={{8,0},{16,8},{24,16},{32,24},{40,32},{48,40},{56,48},{64,56},{72,6... | collective-permute-start | bytes 1179656 | tf_op jit(solution)/shard_map/ppermute | solution.py:10
  25.9 4.2 %collective-permute-start.3 = (bf16[3,256,256]{2,1,0:T(8,128)(2,1)S(1)}, bf16[3,256,256]{2,1,0:T(8,128)(2,1)S(1)}, u32[]{:S(2)}, u32[]{:S(2)}) collective-permute-start(bf16[3,256,256]{2,1,0:T(8,128)(2,1)S(1)} %broadcast_multiply_fusion), channel_id=1, source_target_pairs={{16,0},{24,8},{32,16},{40,24},{48,32},{56,40},{64,48},{72,56},{80,... | collective-permute-start | bytes 1179656 | tf_op jit(solution)/shard_map/ppermute | solution.py:10
  30.2 0.7 compare_and_fusion
  30.8 1.7 %collective-permute-done = bf16[3,256,256]{2,1,0:T(8,128)(2,1)S(1)} collective-permute-done((bf16[3,256,256]{2,1,0:T(8,128)(2,1)S(1)}, bf16[3,256,256]{2,1,0:T(8,128)(2,1)S(1)}, u32[]{:S(2)}, u32[]{:S(2)}) %collective-permute-start) | collective-permute-done | bytes 393248 | tf_op jit(solution)/shard_map/ppermute | solution.py:10
  32.6 0.8 bitcast_dynamic-update-slice_fusion.4
  33.3 2.6 %collective-permute-done.1 = bf16[3,256,256]{2,1,0:T(8,128)(2,1)S(1)} collective-permute-done((bf16[3,256,256]{2,1,0:T(8,128)(2,1)S(1)}, bf16[3,256,256]{2,1,0:T(8,128)(2,1)S(1)}, u32[]{:S(2)}, u32[]{:S(2)}) %collective-permute-start.1) | collective-permute-done | bytes 393248 | tf_op jit(solution)/shard_map/ppermute | solution.py:10
  36.0 0.8 bitcast_dynamic-update-slice_fusion.3
  36.7 0.0 copy-done.1
  36.8 0.8 bitcast_dynamic-update-slice_fusion.2
  37.6 0.0 collective-permute-done.2
  37.6 0.8 bitcast_dynamic-update-slice_fusion.1
  38.4 1.3 %collective-permute-done.3 = bf16[3,256,256]{2,1,0:T(8,128)(2,1)S(1)} collective-permute-done((bf16[3,256,256]{2,1,0:T(8,128)(2,1)S(1)}, bf16[3,256,256]{2,1,0:T(8,128)(2,1)S(1)}, u32[]{:S(2)}, u32[]{:S(2)}) %collective-permute-start.3) | collective-permute-done | bytes 393248 | tf_op jit(solution)/shard_map/ppermute | solution.py:10
  39.6 0.8 bitcast_dynamic-update-slice_fusion
  40.4 5.2 %gather_fusion = bf16[16,3,256,256]{3,2,1,0:T(8,128)(2,1)} fusion(bf16[5,3,256,256]{3,2,1,0:T(8,128)(2,1)} %bitcast_dynamic-update-slice_fusion, s32[1024]{0:T(1024)S(1)} %pad_clamp_fusion), kind=kCustom, calls=%fused_computation | custom fusion | bytes 12582976 | tf_op jit(solution)/shard_map/jit(_take)/gather | solution.py:27
  45.6 0.0 copy-done
  45.6 7.9 %fusion.12 = f32[3,256,256]{2,1,0:T(8,128)} fusion(bf16[16,1,256,256]{3,2,1,0:T(8,128)(2,1)S(1)} %copy-done, bf16[16,1,256,256]{3,2,1,0:T(8,128)(2,1)} %param.7, bf16[16,3,256,256]{3,2,1,0:T(8,128)(2,1)} %gather_fusion, pred[16]{0:T(512)(128)(4,1)S(1)} %get-tuple-element.5), kind=kOutput, calls=%fused_computation.9 | convolution fusion | flops 3227516928 | bytes 11272208 | tf_op jit(solution)/shard_map/kvac,kdc->vad/dot_general | solution.py:31
  53.5 0.0 reduce-scatter.2.cloned.1.call-update
  53.5 0.1 dynamic_slice.12
  53.6 0.1 and_convert_fusion.1
  53.7 41.8 %reduce-scatter.2.cloned.1.call-done = f32[3,32,256]{2,1,0:T(8,128)} async-done(((f32[3,256,256]{2,1,0:T(8,128)}), f32[3,32,256]{2,1,0:T(8,128)}) %reduce-scatter.2.cloned.1.call-update) | async-done | bytes 98320 | tf_op jit(solution)/shard_map/reduce_scatter | solution.py:34
  95.4 1.5 %multiply_convert_fusion = bf16[3,32,256]{2,1,0:T(8,128)(2,1)} fusion(f32[3,32,256]{2,1,0:T(8,128)} %reduce-scatter.2.cloned.1.call-done, f32[32,256]{1,0:T(8,128)S(1)} %and_convert_fusion.1), kind=kLoop, calls=%fused_computation.17 | loop fusion | flops 49152 | bytes 180224 | tf_op jit(solution)/shard_map/convert_element_type | solution.py:38
  (1 shorter events, 0.0 us)
Async XLA Ops:
  6.5 39.1 %copy-start = (bf16[16,1,256,256]{3,2,1,0:T(8,128)(2,1)S(1)}, bf16[16,1,256,256]{3,2,1,0:T(8,128)(2,1)}, u32[]{:S(2)}) copy-start(bf16[16,1,256,256]{3,2,1,0:T(8,128)(2,1)} %param.8) | copy-start | bytes 6291460
  6.5 30.2 %copy-start.1 = (bf16[3,256,256]{2,1,0:T(8,128)(2,1)S(1)}, bf16[3,256,256]{2,1,0:T(8,128)(2,1)}, u32[]{:S(2)}) copy-start(bf16[3,256,256]{2,1,0:T(8,128)(2,1)} %param.6) | copy-start | bytes 1179652
  6.5 88.9 %reduce-scatter.2.cloned.1.call-start = ((), (), s32[]{:S(2)}) async-start(), calls=%async_computation.1 | async-start | bytes 884736 | tf_op jit(solution)/shard_map/reduce_scatter | solution.py:34
  11.7 20.9 %collective-permute-start = (bf16[3,256,256]{2,1,0:T(8,128)(2,1)S(1)}, bf16[3,256,256]{2,1,0:T(8,128)(2,1)S(1)}, u32[]{:S(2)}, u32[]{:S(2)}) collective-permute-start(bf16[3,256,256]{2,1,0:T(8,128)(2,1)S(1)} %broadcast_multiply_fusion), channel_id=1, source_target_pairs={{0,16},{8,24},{16,32},{24,40},{32,48},{40,56},{48,64},{56,72},{64,... | collective-permute-start | bytes 1179656 | tf_op jit(solution)/shard_map/ppermute | solution.py:10
  16.0 20.0 %collective-permute-start.1 = (bf16[3,256,256]{2,1,0:T(8,128)(2,1)S(1)}, bf16[3,256,256]{2,1,0:T(8,128)(2,1)S(1)}, u32[]{:S(2)}, u32[]{:S(2)}) collective-permute-start(bf16[3,256,256]{2,1,0:T(8,128)(2,1)S(1)} %broadcast_multiply_fusion), channel_id=1, source_target_pairs={{0,8},{8,16},{16,24},{24,32},{32,40},{40,48},{48,56},{56,64},{64,7... | collective-permute-start | bytes 1179656 | tf_op jit(solution)/shard_map/ppermute | solution.py:10
  17.9 19.7 %collective-permute-start.2 = (bf16[3,256,256]{2,1,0:T(8,128)(2,1)S(1)}, bf16[3,256,256]{2,1,0:T(8,128)(2,1)S(1)}, u32[]{:S(2)}, u32[]{:S(2)}) collective-permute-start(bf16[3,256,256]{2,1,0:T(8,128)(2,1)S(1)} %broadcast_multiply_fusion), channel_id=1, source_target_pairs={{8,0},{16,8},{24,16},{32,24},{40,32},{48,40},{56,48},{64,56},{72,6... | collective-permute-start | bytes 1179656 | tf_op jit(solution)/shard_map/ppermute | solution.py:10
  25.9 13.7 %collective-permute-start.3 = (bf16[3,256,256]{2,1,0:T(8,128)(2,1)S(1)}, bf16[3,256,256]{2,1,0:T(8,128)(2,1)S(1)}, u32[]{:S(2)}, u32[]{:S(2)}) collective-permute-start(bf16[3,256,256]{2,1,0:T(8,128)(2,1)S(1)} %broadcast_multiply_fusion), channel_id=1, source_target_pairs={{16,0},{24,8},{32,16},{40,24},{48,32},{56,40},{64,48},{72,56},{80,... | collective-permute-start | bytes 1179656 | tf_op jit(solution)/shard_map/ppermute | solution.py:10
Sparse Core Ops, SparseCore 0:
  53.6 41.7 reduce-scatter.1
where the time goes:
time: 104 us
  waiting for transfers between devices  47.4 us (46%)
  starting transfers between devices  18.4 us (18%)
  between operations  13.5 us (13%)
  local copies, waits for them, and re-layouts  11.1 us (11%)
  matrix products  7.86 us (8%)
  other arithmetic  5.57 us (5%)
    reduce_scatter x1, waiting for transfers between devices, per_device(): lax.psum_scatter(partial_value, 'term', scatter_dimension=1, tiled=True)  41.8 us
    ppermute x4, starting transfers between devices, from_behind(): return lax.ppermute(value, axis, pairs)  18.4 us
    dot_general x1, matrix products, per_device(): jnp.einsum('kvac,kdc->vad', products, right_blocks[:, 0], preferred_eleme...  7.86 us
    ppermute x4, waiting for transfers between devices, from_behind(): return lax.ppermute(value, axis, pairs)  5.64 us
    gather x1, local copies, waits for them, and re-layouts, per_device(): selected = jnp.take(sources, term_shift + 2, axis=0)  5.16 us
    unnamed x7, local copies, waits for them, and re-layouts  2.34 us
  transfers between devices with their start and end apart: 5, of which 4 were waited for; matrix products, arithmetic and copies ran while one was open for 4% of the time, Pallas kernels for 0%

commit v1 on v0

v1 whole, which is shorter than its diff:
```python
import jax
import jax.numpy as jnp
from jax import lax
from jax.experimental import pallas as pl
from jax.experimental.pallas import tpu as pltpu
from jax.sharding import PartitionSpec as P

MESH = pl.DeviceIdType.MESH
F32, BF16 = jnp.float32, jnp.bfloat16
ROWS_BY_ROWS = (((1,), (1,)), ((), ()))
PEERS = (4, 3, 5, 2, 6, 1, 7)


def kernel(
    sectors, groups,
    wave_hbm, left_hbm, right_hbm, shift_hbm, lsize_hbm, rsize_hbm,
    out_ref,
    wave, src0, src1, src2, left, right, prod, total, part, landed, shift, lsize, rsize,
    load_sem, z_send, z_recv, c_send, c_recv, f_send, f_recv, y_send, y_recv,
):
    vecs, rows, cols = wave.shape
    terms = left.shape[0]
    piece = rows // groups
    src = (src0, src1, src2)
    s = lax.axis_index("sec")
    t = lax.axis_index("term")
    core = lax.rem(s, 2)
    twin = s + 1 - 2 * core
    up = lax.rem(s + 2, sectors)
    down = lax.rem(s + sectors - 2, sectors)

    def peer(d):
        return lax.rem(t + d, groups)

    barrier = pltpu.get_barrier_semaphore()
    for place in ((twin, t), (up, t), (down, t), *((s, peer(d)) for d in PEERS)):
        pl.semaphore_signal(barrier, inc=1, device_id=place, device_id_type=MESH)

    loads = [
        pltpu.make_async_copy(lsize_hbm, lsize, load_sem.at[0]),
        pltpu.make_async_copy(rsize_hbm, rsize, load_sem.at[1]),
        pltpu.make_async_copy(wave_hbm, wave, load_sem.at[2]),
        pltpu.make_async_copy(shift_hbm, shift, load_sem.at[3]),
        pltpu.make_async_copy(left_hbm.at[:, 0], left, load_sem.at[4]),
    ]
    loads += [
        pltpu.make_async_copy(right_hbm.at[k, 0], right.at[:, pl.ds(k * cols, cols)], load_sem.at[5 + k])
        for k in range(terms)
    ]
    for load in loads:
        load.start()

    for v in range(vecs):
        src[v][5] = jnp.zeros((rows, cols), BF16)
    loads[0].wait()
    loads[1].wait()
    row_at = lax.broadcasted_iota(jnp.int32, (rows, cols), 0)
    col_at = lax.broadcasted_iota(jnp.int32, (rows, cols), 1)
    valid = jnp.where((row_at < lsize[s]) & (col_at < rsize[s]), 1.0, 0.0).astype(F32)
    loads[2].wait()
    for v in range(vecs):
        src[v][2] = wave[v] * valid.astype(BF16)
    pl.semaphore_wait(barrier, 3 + len(PEERS))

    up_from = jnp.where(s + 2 >= sectors, 5, 2)
    down_from = jnp.where(s < 2, 5, 2)
    first_to = jnp.where(core == 1, up, down)
    first_from = jnp.where(core == 1, up_from, down_from)
    first_slot = 4 * (1 - core)
    second_to = jnp.where(core == 1, down, up)
    second_from = jnp.where(core == 1, down_from, up_from)
    second_slot = 4 * core

    def first(v):
        return pltpu.make_async_remote_copy(
            src_ref=src[v].at[first_from], dst_ref=src[v].at[first_slot], send_sem=z_send.at[0, v], recv_sem=z_recv.at[0, v],
            device_id=(first_to, t), device_id_type=MESH)

    def second(v):
        return pltpu.make_async_remote_copy(
            src_ref=src[v].at[second_from], dst_ref=src[v].at[second_slot], send_sem=z_send.at[1, v], recv_sem=z_recv.at[1, v],
            device_id=(second_to, t), device_id_type=MESH)

    def own(v):
        return pltpu.make_async_remote_copy(
            src_ref=src[v].at[2], dst_ref=src[v].at[1 + 2 * core], send_sem=c_send.at[v], recv_sem=c_recv.at[v],
            device_id=(twin, t), device_id_type=MESH)

    def onward(v):
        return pltpu.make_async_remote_copy(
            src_ref=src[v].at[first_slot], dst_ref=src[v].at[3 - 2 * core], send_sem=f_send.at[v], recv_sem=f_recv.at[v],
            device_id=(twin, t), device_id_type=MESH)

    def share(v, d):
        there = pl.multiple_of(peer(d) * piece, piece)
        return pltpu.make_async_remote_copy(
            src_ref=part.at[v, pl.ds(there, piece)], dst_ref=landed.at[v, d - 1], send_sem=y_send.at[v, d - 1], recv_sem=y_recv.at[v, d - 1],
            device_id=(s, peer(d)), device_id_type=MESH)

    for v in range(vecs):
        first(v).start()
        second(v).start()
    for v in range(vecs):
        own(v).start()
    for load in loads[3:]:
        load.wait()

    for v in range(vecs):
        first(v).wait_recv()
        onward(v).start()
        own(v).wait_recv()
        second(v).wait_recv()
        onward(v).wait_recv()
        for k in range(terms):
            prod[:, k * cols:(k + 1) * cols] = jnp.dot(
                left[k], src[v][shift[k] + 2], preferred_element_type=F32
            ).astype(BF16)
        summed = lax.dot_general(prod[...], right[...], ROWS_BY_ROWS, preferred_element_type=F32) * valid
        total[v] = summed
        part[v] = summed.astype(BF16)
        for d in PEERS:
            share(v, d).start()

    mine = pl.multiple_of(t * piece, piece)
    for v in range(vecs):
        result = total[v, pl.ds(mine, piece)]
        for d in PEERS[::-1]:
            share(v, d).wait_recv()
            result = result + landed[v, d - 1].astype(F32)
        out_ref[v] = result.astype(BF16)
    for v in range(vecs):
        first(v).wait_send()
        second(v).wait_send()
        own(v).wait_send()
        onward(v).wait_send()
        for d in PEERS:
            share(v, d).wait_send()


def solution(mesh):
    sectors, groups = mesh.shape["sec"], mesh.shape["term"]

    def per_device(wave, left, right, shift, lsize, rsize):
        vecs, rows, cols = wave.shape
        terms = left.shape[0]
        piece = rows // groups
        far = len(PEERS)

        def body(*refs):
            kernel(sectors, groups, *refs)

        dma = pltpu.SemaphoreType.DMA
        return pl.pallas_call(
            body,
            name="sigma",
            out_shape=jax.ShapeDtypeStruct((vecs, piece, cols), BF16),
            in_specs=[pl.BlockSpec(memory_space=pltpu.HBM)] * 6,
            out_specs=pl.BlockSpec(memory_space=pltpu.VMEM),
            scratch_shapes=[
                pltpu.VMEM((vecs, rows, cols), BF16),
                *[pltpu.VMEM((6, rows, cols), BF16) for _ in range(vecs)],
                pltpu.VMEM((terms, rows, rows), BF16),
                pltpu.VMEM((cols, terms * cols), BF16),
                pltpu.VMEM((rows, terms * cols), BF16),
                pltpu.VMEM((vecs, rows, cols), F32),
                pltpu.VMEM((vecs, rows, cols), BF16),
                pltpu.VMEM((vecs, far, piece, cols), BF16),
                pltpu.SMEM(shift.shape, jnp.int32),
                pltpu.SMEM(lsize.shape, jnp.int32),
                pltpu.SMEM(rsize.shape, jnp.int32),
                dma((5 + terms,)),
                dma((2, vecs)), dma((2, vecs)),
                dma((vecs,)), dma((vecs,)),
                dma((vecs,)), dma((vecs,)),
                dma((vecs, far)), dma((vecs, far)),
            ],
            compiler_params=pltpu.CompilerParams(
                collective_id=0, has_side_effects=True, vmem_limit_bytes=60 * 2**20
            ),
        )(wave, left, right, shift, lsize, rsize)

    return jax.shard_map(
        per_device,
        mesh=mesh,
        in_specs=(P(None, "sec", None), P("term", "sec", None, None), P("term", "sec", None, None), P("term"), P(), P()),
        out_specs=P(None, ("sec", "term"), None),
        check_vma=False,
    )
```

time: 104 us -> 37.5 us (0.36)
  the two profiles are of different devices: /device:TPU:2 before, /device:TPU:1 now
where the time goes in v1:
time: 37.5 us; the launch traced here: 37.3 us
  Pallas kernels  35.9 us (96%)
  local copies, waits for them, and re-layouts  1.42 us (4%)
    pallas_call x1, Pallas kernels, per_device(): pl.pallas_call(body, name='sigma', out_shape=jax.ShapeDtypeStruct((vecs,...  35.9 us
    unnamed x1, local copies, waits for them, and re-layouts  1.42 us

profile of v1, /device:TPU:1, one launch (start us, length us, event | category | flops | bytes accessed | tf_op | source)
XLA Modules:
  0.0 37.3 jit_solution(13570936021735145446)
XLA Ops:
  0.0 35.9 %sigma.1 = bf16[3,32,256]{2,1,0:T(8,128)(2,1)} custom-call(bf16[3,256,256]{2,1,0:T(8,128)(2,1)} %refs_0_.1, bf16[16,1,256,256]{3,2,1,0:T(8,128)(2,1)} %refs_1_.1, bf16[16,1,256,256]{3,2,1,0:T(8,128)(2,1)} %refs_2_.1, s32[16]{0:T(128)} %refs_3_.1, s32[64]{0:T(128)} %refs_4_.1, s32[64]{0:T(128)} %refs_5_.1), custom_call_target="tpu_custom_call" | custom-call | tf_op jit(solution)/shard_map/sigma/pallas_call | solution.py:153
  35.9 1.4 %copy.8 = bf16[3,32,256]{2,1,0:T(8,128)(2,1)} copy(bf16[3,32,256]{2,1,0:T(8,128)(2,1)} %sigma.1) | data formatting | bytes 98304

commit v2 on v1

v2 whole, which is shorter than its diff:
```python
import jax
import jax.numpy as jnp
from jax import lax
from jax.experimental import pallas as pl
from jax.experimental.pallas import tpu as pltpu
from jax.sharding import PartitionSpec as P

MESH = pl.DeviceIdType.MESH
F32, BF16 = jnp.float32, jnp.bfloat16
ROWS_BY_ROWS = (((1,), (1,)), ((), ()))
LINE = 8
PEERS = (4, 3, 5, 2, 6, 1, 7)


def kernel(
    sectors, groups,
    wave_hbm, left_hbm, right_hbm, shift_hbm, lsize_hbm, rsize_hbm,
    out_ref,
    src0, src1, src2, left, right, prod, masked, mask, total, part, landed, shift, lsize, rsize,
    load_sem, z_send, z_recv, c_send, c_recv, f_send, f_recv, y_send, y_recv, told,
):
    vecs, rows, cols = total.shape
    terms = left.shape[0]
    piece = rows // groups
    src = (src0, src1, src2)
    s = lax.axis_index("sec")
    t = lax.axis_index("term")
    core = lax.rem(s, 2)
    twin = s + 1 - 2 * core
    up = lax.rem(s + 2, sectors)
    down = lax.rem(s + sectors - 2, sectors)

    def peer(d):
        return lax.rem(t + d, groups)

    barrier = pltpu.get_barrier_semaphore()
    def greet(sem, place):
        pl.semaphore_signal(sem, inc=1, device_id=place, device_id_type=MESH)

    at = lax.rem(s // 2, LINE)
    last, before = at == LINE - 1, at == LINE - 2
    for place in ((twin, t), (up, t), (down, t)):
        greet(barrier, place)

    @pl.when(jnp.logical_not(last))
    def _():
        for d in PEERS:
            greet(barrier, (s, peer(d)))

    first_to = jnp.where(core == 1, up, down)
    first_slot = 4 * (1 - core)
    second_to = jnp.where(core == 1, down, up)
    second_slot = 4 * core
    own_slot = 1 + 2 * core
    onward_slot = 3 - 2 * core

    def first(v):
        return pltpu.make_async_remote_copy(
            src_ref=wave_hbm.at[v], dst_ref=src[v].at[first_slot], send_sem=z_send.at[0, v], recv_sem=z_recv.at[0, v],
            device_id=(first_to, t), device_id_type=MESH)

    def second(v):
        return pltpu.make_async_remote_copy(
            src_ref=wave_hbm.at[v], dst_ref=src[v].at[second_slot], send_sem=z_send.at[1, v], recv_sem=z_recv.at[1, v],
            device_id=(second_to, t), device_id_type=MESH)

    def own(v):
        return pltpu.make_async_remote_copy(
            src_ref=wave_hbm.at[v], dst_ref=src[v].at[own_slot], send_sem=c_send.at[v], recv_sem=c_recv.at[v],
            device_id=(twin, t), device_id_type=MESH)

    def onward(v):
        return pltpu.make_async_remote_copy(
            src_ref=src[v].at[first_slot], dst_ref=src[v].at[onward_slot], send_sem=f_send.at[v], recv_sem=f_recv.at[v],
            device_id=(twin, t), device_id_type=MESH)

    def share(v, d):
        there = pl.multiple_of(peer(d) * piece, piece)
        return pltpu.make_async_remote_copy(
            src_ref=part.at[v, pl.ds(there, piece)], dst_ref=landed.at[v, d - 1], send_sem=y_send.at[v, d - 1], recv_sem=y_recv.at[v, d - 1],
            device_id=(s, peer(d)), device_id_type=MESH)

    @pl.when(last)
    def _():
        pl.semaphore_wait(barrier, 3)

    @pl.when(jnp.logical_not(last))
    def _():
        pl.semaphore_wait(barrier, 3 + len(PEERS))

    for v in range(vecs):
        first(v).start()
        second(v).start()
    for v in range(vecs):
        own(v).start()

    loads = [
        pltpu.make_async_copy(lsize_hbm, lsize, load_sem.at[0]),
        pltpu.make_async_copy(rsize_hbm, rsize, load_sem.at[1]),
        pltpu.make_async_copy(shift_hbm, shift, load_sem.at[2]),
        pltpu.make_async_copy(left_hbm.at[:, 0], left, load_sem.at[3]),
    ]
    loads += [pltpu.make_async_copy(wave_hbm.at[v], src[v].at[2], load_sem.at[4 + v]) for v in range(vecs)]
    loads += [
        pltpu.make_async_copy(right_hbm.at[k, 0], right.at[:, pl.ds(k * cols, cols)], load_sem.at[4 + vecs + k])
        for k in range(terms)
    ]
    for load in loads:
        load.start()

    loads[0].wait()
    loads[1].wait()
    row_at = lax.broadcasted_iota(jnp.int32, (rows, cols), 0)
    col_at = lax.broadcasted_iota(jnp.int32, (rows, cols), 1)
    for o in range(5):
        q = s + o - 2
        inside = (q >= 0) & (q < sectors)
        q = jnp.clip(q, 0, sectors - 1)
        limit = jnp.where(inside, lsize[q], 0)
        mask[o] = jnp.where((row_at < limit) & (col_at < rsize[q]), 1.0, 0.0).astype(BF16)
    for load in loads[2:]:
        load.wait()

    @pl.when(before)
    def _():
        for d in PEERS:
            greet(told, (s, peer(d)))
        pl.semaphore_wait(told, len(PEERS))
        greet(told, (up, t))

    def admit(v, slot):
        masked[slot] = src[v][slot] * mask[slot]

    for v in range(vecs):
        admit(v, 2)
        first(v).wait_recv()
        onward(v).start()
        own(v).wait_recv()
        admit(v, onward_slot)
        admit(v, first_slot)
        second(v).wait_recv()
        admit(v, second_slot)
        onward(v).wait_recv()
        admit(v, own_slot)
        for k in range(terms):
            prod[:, k * cols:(k + 1) * cols] = jnp.dot(
                left[k], masked[shift[k] + 2], preferred_element_type=F32
            ).astype(BF16)
        summed = lax.dot_general(prod[...], right[...], ROWS_BY_ROWS, preferred_element_type=F32) * mask[2].astype(F32)
        total[v] = summed
        part[v] = summed.astype(BF16)
        if v == 0:
            @pl.when(last)
            def _():
                pl.semaphore_wait(told, 1)

        for d in PEERS:
            share(v, d).start()

    for v in range(vecs):
        first(v).wait_send()
        second(v).wait_send()
        own(v).wait_send()
        onward(v).wait_send()
        for d in PEERS:
            share(v, d).wait_send()
    for v in range(vecs):
        result = total[v, pl.ds(pl.multiple_of(t * piece, piece), piece)]
        for d in PEERS[::-1]:
            share(v, d).wait_recv()
            result = result + landed[v, d - 1].astype(F32)
        out_ref[v] = result.astype(BF16)


def solution(mesh):
    sectors, groups = mesh.shape["sec"], mesh.shape["term"]

    def per_device(wave, left, right, shift, lsize, rsize):
        vecs, rows, cols = wave.shape
        terms = left.shape[0]
        piece = rows // groups
        far = len(PEERS)

        def body(*refs):
            kernel(sectors, groups, *refs)

        dma = pltpu.SemaphoreType.DMA
        return pl.pallas_call(
            body,
            name="sigma",
            out_shape=jax.ShapeDtypeStruct((vecs, piece, cols), BF16),
            in_specs=[pl.BlockSpec(memory_space=pltpu.HBM)] * 6,
            out_specs=pl.BlockSpec(memory_space=pltpu.VMEM),
            scratch_shapes=[
                *[pltpu.VMEM((5, rows, cols), BF16) for _ in range(vecs)],
                pltpu.VMEM((terms, rows, rows), BF16),
                pltpu.VMEM((cols, terms * cols), BF16),
                pltpu.VMEM((rows, terms * cols), BF16),
                pltpu.VMEM((5, rows, cols), BF16),
                pltpu.VMEM((5, rows, cols), BF16),
                pltpu.VMEM((vecs, rows, cols), F32),
                pltpu.VMEM((vecs, rows, cols), BF16),
                pltpu.VMEM((vecs, far, piece, cols), BF16),
                pltpu.SMEM(shift.shape, jnp.int32),
                pltpu.SMEM(lsize.shape, jnp.int32),
                pltpu.SMEM(rsize.shape, jnp.int32),
                dma((4 + vecs + terms,)),
                dma((2, vecs)), dma((2, vecs)),
                dma((vecs,)), dma((vecs,)),
                dma((vecs,)), dma((vecs,)),
                dma((vecs, far)), dma((vecs, far)),
                pltpu.SemaphoreType.REGULAR,
            ],
            compiler_params=pltpu.CompilerParams(
                collective_id=0, has_side_effects=True, vmem_limit_bytes=60 * 2**20
            ),
        )(wave, left, right, shift, lsize, rsize)

    return jax.shard_map(
        per_device,
        mesh=mesh,
        in_specs=(P(None, "sec", None), P("term", "sec", None, None), P("term", "sec", None, None), P("term"), P(), P()),
        out_specs=P(None, ("sec", "term"), None),
        check_vma=False,
    )
```

time: 37.5 us -> 35.6 us (0.949)
  Pallas kernels: 35.9 us -> 34 us
    pallas_call x1, Pallas kernels: 35.9 us -> 34 us  [per_device(): pl.pallas_call(body, name='sigma', out_shape=jax.ShapeDtypeStruct((vecs,...]
where the time goes in v2:
time: 35.6 us; the launch traced here: 35.5 us
  Pallas kernels  34 us (96%)
  local copies, waits for them, and re-layouts  1.42 us (4%)
    pallas_call x1, Pallas kernels, per_device(): pl.pallas_call(body, name='sigma', out_shape=jax.ShapeDtypeStruct((vecs,...  34 us
    unnamed x1, local copies, waits for them, and re-layouts  1.42 us

profile of v2, /device:TPU:1, one launch (start us, length us, event | category | flops | bytes accessed | tf_op | source)
XLA Modules:
  0.0 35.5 jit_solution(14314288630671604371)
XLA Ops:
  0.0 34.0 %sigma.1 = bf16[3,32,256]{2,1,0:T(8,128)(2,1)} custom-call(bf16[3,256,256]{2,1,0:T(8,128)(2,1)} %refs_0_.1, bf16[16,1,256,256]{3,2,1,0:T(8,128)(2,1)} %refs_1_.1, bf16[16,1,256,256]{3,2,1,0:T(8,128)(2,1)} %refs_2_.1, s32[16]{0:T(128)} %refs_3_.1, s32[64]{0:T(128)} %refs_4_.1, s32[64]{0:T(128)} %refs_5_.1), custom_call_target="tpu_custom_call" | custom-call | tf_op jit(solution)/shard_map/sigma/pallas_call | solution.py:188
  34.0 1.4 %copy.8 = bf16[3,32,256]{2,1,0:T(8,128)(2,1)} copy(bf16[3,32,256]{2,1,0:T(8,128)(2,1)} %sigma.1) | data formatting | bytes 98304

commit v3 on v2

--- a/solution.py
+++ b/solution.py
@@ -17,7 +17,7 @@
     wave_hbm, left_hbm, right_hbm, shift_hbm, lsize_hbm, rsize_hbm,
     out_ref,
     src0, src1, src2, left, right, prod, masked, mask, total, part, landed, shift, lsize, rsize,
-    load_sem, z_send, z_recv, c_send, c_recv, f_send, f_recv, y_send, y_recv, told,
+    load_sem, z_send, z_recv, c_send, c_recv, f_send, f_recv, y_send, y_recv, told, near,
 ):
     vecs, rows, cols = total.shape
     terms = left.shape[0]
@@ -27,8 +27,10 @@
     t = lax.axis_index("term")
     core = lax.rem(s, 2)
     twin = s + 1 - 2 * core
-    up = lax.rem(s + 2, sectors)
-    down = lax.rem(s + sectors - 2, sectors)
+    up, down = s + 2, s - 2
+    has_up, has_down = up < sectors, down >= 0
+    beside = s + 2 * core - 1
+    along = has_up.astype(jnp.int32) + has_down.astype(jnp.int32) + jnp.where(core == 1, has_up, has_down).astype(jnp.int32)
 
     def peer(d):
         return lax.rem(t + d, groups)
@@ -39,8 +41,23 @@
 
     at = lax.rem(s // 2, LINE)
     last, before = at == LINE - 1, at == LINE - 2
-    for place in ((twin, t), (up, t), (down, t)):
-        greet(barrier, place)
+    after = (at == 0) & has_down
+    pl.when(jnp.logical_not(last))(lambda: greet(barrier, (twin, t)))
+
+    @pl.when(has_up & jnp.logical_not(last | before))
+    def _():
+        greet(barrier, (up, t))
+
+    @pl.when(has_down)
+    def _():
+        greet(barrier, (down, t))
+
+    first_up = core == 1
+    first_goes = jnp.where(first_up, has_up, has_down)
+
+    @pl.when(first_goes & jnp.logical_not((last | before) & first_up))
+    def _():
+        greet(barrier, (beside, t))
 
     @pl.when(jnp.logical_not(last))
     def _():
@@ -53,6 +70,8 @@
     second_slot = 4 * core
     own_slot = 1 + 2 * core
     onward_slot = 3 - 2 * core
+    second_goes = jnp.where(core == 1, has_down, has_up)
+    first_comes, second_comes = second_goes, first_goes
 
     def first(v):
         return pltpu.make_async_remote_copy(
@@ -74,6 +93,12 @@
             src_ref=src[v].at[first_slot], dst_ref=src[v].at[onward_slot], send_sem=f_send.at[v], recv_sem=f_recv.at[v],
             device_id=(twin, t), device_id_type=MESH)
 
+    def relay():
+        v = vecs - 1
+        return pltpu.make_async_remote_copy(
+            src_ref=src[v].at[onward_slot], dst_ref=src[v].at[first_slot], send_sem=z_send.at[1, v], recv_sem=z_recv.at[1, v],
+            device_id=(beside, t), device_id_type=MESH)
+
     def share(v, d):
         there = pl.multiple_of(peer(d) * piece, piece)
         return pltpu.make_async_remote_copy(
@@ -82,17 +107,45 @@
 
     @pl.when(last)
     def _():
-        pl.semaphore_wait(barrier, 3)
+        @pl.when(has_up)
+        def _():
+            pl.semaphore_wait(barrier, 1 + core)
+
+        @pl.when(has_up)
+        def _():
+            greet(told, (up, t))
+
+        @pl.when(has_up & first_up)
+        def _():
+            greet(told, (beside, t))
 
     @pl.when(jnp.logical_not(last))
     def _():
-        pl.semaphore_wait(barrier, 3 + len(PEERS))
-
-    for v in range(vecs):
-        first(v).start()
-        second(v).start()
-    for v in range(vecs):
+        pl.semaphore_wait(barrier, 1 + along - jnp.where(after, 2 - core, 0) + len(PEERS))
+
+    for v in range(vecs):
+        pl.when(first_goes & jnp.logical_not((after | last) & (core == 0)))(first(v).start)
+        if v < vecs - 1:
+            pl.when(second_goes & jnp.logical_not((after | last) & (core == 1)))(second(v).start)
+
+    @pl.when(before)
+    def _():
+        greet(near, (up, t))
+        pl.when(core == 1)(lambda: greet(near, (beside, t)))
+
+    @pl.when(last)
+    def _():
+        pl.semaphore_wait(near, 2 - core)
+
+    for v in range(vecs):
+        pl.when(last & (core == 0))(first(v).start)
+        if v < vecs - 1:
+            pl.when(last & (core == 1))(second(v).start)
+    for v in range(vecs - 1, -1, -1):
         own(v).start()
+
+    own(vecs - 1).wait_recv()
+    pl.when(first_goes & jnp.logical_not(after & (core == 0)))(relay().start)
 
     loads = [
         pltpu.make_async_copy(lsize_hbm, lsize, load_sem.at[0]),
@@ -121,6 +174,16 @@
     for load in loads[2:]:
         load.wait()
 
+    @pl.when(after)
+    def _():
+        pl.semaphore_wait(told, 2 - core)
+
+    for v in range(vecs):
+        pl.when(after & (core == 0))(first(v).start)
+        if v < vecs - 1:
+            pl.when(after & (core == 1))(second(v).start)
+    pl.when(after & (core == 0))(relay().start)
+
     @pl.when(before)
     def _():
         for d in PEERS:
@@ -131,17 +194,37 @@
     def admit(v, slot):
         masked[slot] = src[v][slot] * mask[slot]
 
+    @pl.when(jnp.logical_not(first_comes))
+    def _():
+        masked[first_slot] = jnp.zeros((rows, cols), BF16)
+
+    @pl.when(jnp.logical_not(second_comes))
+    def _():
+        masked[second_slot] = jnp.zeros((rows, cols), BF16)
+        masked[own_slot] = jnp.zeros((rows, cols), BF16)
+
     for v in range(vecs):
         admit(v, 2)
-        first(v).wait_recv()
-        onward(v).start()
-        own(v).wait_recv()
+        @pl.when(first_comes)
+        def _():
+            first(v).wait_recv()
+            onward(v).start()
+
+        if v < vecs - 1:
+            own(v).wait_recv()
         admit(v, onward_slot)
-        admit(v, first_slot)
-        second(v).wait_recv()
-        admit(v, second_slot)
-        onward(v).wait_recv()
-        admit(v, own_slot)
+
+        @pl.when(first_comes)
+        def _():
+            admit(v, first_slot)
+
+        @pl.when(second_comes)
+        def _():
+            second(v).wait_recv() if v < vecs - 1 else relay().wait_recv()
+            admit(v, second_slot)
+            onward(v).wait_recv()
+            admit(v, own_slot)
+
         for k in range(terms):
             prod[:, k * cols:(k + 1) * cols] = jnp.dot(
                 left[k], masked[shift[k] + 2], preferred_element_type=F32
@@ -158,13 +241,17 @@
             share(v, d).start()
 
     for v in range(vecs):
-        first(v).wait_send()
-        second(v).wait_send()
         own(v).wait_send()
-        onward(v).wait_send()
-        for d in PEERS:
-            share(v, d).wait_send()
-    for v in range(vecs):
+        pl.when(first_goes)(first(v).wait_send)
+        pl.when(second_goes)(second(v).wait_send) if v < vecs - 1 else pl.when(first_goes)(relay().wait_send)
+        pl.when(first_comes)(onward(v).wait_send)
+        if v < vecs - 1:
+            for d in PEERS:
+                share(v, d).wait_send()
+    for v in range(vecs):
+        if v == vecs - 1:
+            for d in PEERS:
+                share(v, d).wait_send()
         result = total[v, pl.ds(pl.multiple_of(t * piece, piece), piece)]
         for d in PEERS[::-1]:
             share(v, d).wait_recv()
@@ -210,6 +297,7 @@
                 dma((vecs,)), dma((vecs,)),
                 dma((vecs, far)), dma((vecs, far)),
                 pltpu.SemaphoreType.REGULAR,
+                pltpu.SemaphoreType.REGULAR,
             ],
             compiler_params=pltpu.CompilerParams(
                 collective_id=0, has_side_effects=True, vmem_limit_bytes=60 * 2**20

time: 35.6 us -> 32.4 us (0.910)
  the two profiles are of different devices: /device:TPU:1 before, /device:TPU:7 now
where the time goes in v3:
time: 32.4 us; the launch traced here: 32.3 us
  Pallas kernels  30.8 us (95%)
  local copies, waits for them, and re-layouts  1.42 us (4%)
    pallas_call x1, Pallas kernels, per_device(): pl.pallas_call(body, name='sigma', out_shape=jax.ShapeDtypeStruct((vecs,...  30.8 us
    unnamed x1, local copies, waits for them, and re-layouts  1.42 us

profile of v3, /device:TPU:7, one launch (start us, length us, event | category | flops | bytes accessed | tf_op | source)
XLA Modules:
  0.0 32.3 jit_solution(11318881394607442775)
XLA Ops:
  0.0 30.8 %sigma.1 = bf16[3,32,256]{2,1,0:T(8,128)(2,1)} custom-call(bf16[3,256,256]{2,1,0:T(8,128)(2,1)} %refs_0_.1, bf16[16,1,256,256]{3,2,1,0:T(8,128)(2,1)} %refs_1_.1, bf16[16,1,256,256]{3,2,1,0:T(8,128)(2,1)} %refs_2_.1, s32[16]{0:T(128)} %refs_3_.1, s32[64]{0:T(128)} %refs_4_.1, s32[64]{0:T(128)} %refs_5_.1), custom_call_target="tpu_custom_call" | custom-call | tf_op jit(solution)/shard_map/sigma/pallas_call | solution.py:275
  30.8 1.4 %copy.8 = bf16[3,32,256]{2,1,0:T(8,128)(2,1)} copy(bf16[3,32,256]{2,1,0:T(8,128)(2,1)} %sigma.1) | data formatting | bytes 98304

commit v4 on v3

--- a/solution.py
+++ b/solution.py
@@ -42,27 +42,8 @@
     at = lax.rem(s // 2, LINE)
     last, before = at == LINE - 1, at == LINE - 2
     after = (at == 0) & has_down
-    pl.when(jnp.logical_not(last))(lambda: greet(barrier, (twin, t)))
-
-    @pl.when(has_up & jnp.logical_not(last | before))
-    def _():
-        greet(barrier, (up, t))
-
-    @pl.when(has_down)
-    def _():
-        greet(barrier, (down, t))
-
     first_up = core == 1
     first_goes = jnp.where(first_up, has_up, has_down)
-
-    @pl.when(first_goes & jnp.logical_not((last | before) & first_up))
-    def _():
-        greet(barrier, (beside, t))
-
-    @pl.when(jnp.logical_not(last))
-    def _():
-        for d in PEERS:
-            greet(barrier, (s, peer(d)))
 
     first_to = jnp.where(core == 1, up, down)
     first_slot = 4 * (1 - core)
@@ -111,22 +92,45 @@
         def _():
             pl.semaphore_wait(barrier, 1 + core)
 
+            @pl.when(first_up)
+            def _():
+                for v in range(vecs):
+                    first(v).start()
+
+            @pl.when(jnp.logical_not(first_up))
+            def _():
+                for v in range(vecs - 1):
+                    second(v).start()
+
+        greet(barrier, (down, t))
+        pl.when(jnp.logical_not(first_up))(lambda: greet(barrier, (beside, t)))
+
         @pl.when(has_up)
         def _():
             greet(told, (up, t))
-
-        @pl.when(has_up & first_up)
-        def _():
-            greet(told, (beside, t))
+            pl.when(first_up)(lambda: greet(told, (beside, t)))
 
     @pl.when(jnp.logical_not(last))
     def _():
+        greet(barrier, (twin, t))
+        pl.when(has_down)(lambda: greet(barrier, (down, t)))
+
+        @pl.when(has_up & jnp.logical_not(before))
+        def _():
+            greet(barrier, (up, t))
+
+        @pl.when(first_goes & jnp.logical_not(before & first_up))
+        def _():
+            greet(barrier, (beside, t))
+
+        for d in PEERS:
+            greet(barrier, (s, peer(d)))
         pl.semaphore_wait(barrier, 1 + along - jnp.where(after, 2 - core, 0) + len(PEERS))
 
-    for v in range(vecs):
-        pl.when(first_goes & jnp.logical_not((after | last) & (core == 0)))(first(v).start)
-        if v < vecs - 1:
-            pl.when(second_goes & jnp.logical_not((after | last) & (core == 1)))(second(v).start)
+        for v in range(vecs):
+            pl.when(first_goes & jnp.logical_not(after & (core == 0)))(first(v).start)
+            if v < vecs - 1:
+                pl.when(second_goes & jnp.logical_not(after & (core == 1)))(second(v).start)
 
     @pl.when(before)
     def _():
@@ -300,9 +304,9 @@
                 pltpu.SemaphoreType.REGULAR,
             ],
             compiler_params=pltpu.CompilerParams(
-                collective_id=0, has_side_effects=True, vmem_limit_bytes=60 * 2**20
+                collective_id=0, has_side_effects=True, vmem_limit_bytes=48 * 2**20
             ),
-        )(wave, left, right, shift, lsize, rsize)
+        )(*[pltpu.with_memory_space_constraint(x, pltpu.HBM) for x in (wave, left, right, shift, lsize, rsize)])
 
     return jax.shard_map(
         per_device,

time: 32.4 us -> 30.9 us (0.954)
  local copies, waits for them, and re-layouts: 1.42 us -> 0.62 us
  Pallas kernels: 30.8 us -> 30.1 us
    unnamed x1, local copies, waits for them, and re-layouts: 1.42 us -> 0.62 us
    pallas_call x1, Pallas kernels: 30.8 us -> 30.1 us  [per_device(): pl.pallas_call(body, name='sigma', out_shape=jax.ShapeDtypeStruct((vecs,...]
where the time goes in v4:
time: 30.9 us; the launch traced here: 30.8 us
  Pallas kernels  30.1 us (97%)
  local copies, waits for them, and re-layouts  0.62 us (2%)
    pallas_call x1, Pallas kernels, per_device(): pl.pallas_call(body, name='sigma', out_shape=jax.ShapeDtypeStruct((vecs,...  30.1 us
    unnamed x1, local copies, waits for them, and re-layouts  0.62 us

profile of v4, /device:TPU:7, one launch (start us, length us, event | category | flops | bytes accessed | tf_op | source)
XLA Modules:
  0.0 30.8 jit_solution(13307452433277356441)
XLA Ops:
  0.0 30.1 %sigma.1 = bf16[3,32,256]{2,1,0:T(8,128)(2,1)S(1)} custom-call(bf16[3,256,256]{2,1,0:T(8,128)(2,1)} %refs_0_.1, bf16[16,1,256,256]{3,2,1,0:T(8,128)(2,1)} %refs_1_.1, bf16[16,1,256,256]{3,2,1,0:T(8,128)(2,1)} %refs_2_.1, s32[16]{0:T(128)} %refs_3_.1, s32[64]{0:T(128)} %refs_4_.1, s32[64]{0:T(128)} %refs_5_.1), custom_call_target="tpu_custom_call" | custom-call | tf_op jit(solution)/shard_map/sigma/pallas_call | solution.py:279
  30.2 0.6 %copy.8 = bf16[3,32,256]{2,1,0:T(8,128)(2,1)} copy(bf16[3,32,256]{2,1,0:T(8,128)(2,1)S(1)} %sigma.1) | data formatting | bytes 98304

commit v5 on v4

--- a/solution.py
+++ b/solution.py
@@ -178,6 +178,12 @@
     for load in loads[2:]:
         load.wait()
 
+    row_ok = jnp.where(row_at < lsize[s], 1.0, 0.0).astype(BF16)
+    col_ok = jnp.where(row_at < rsize[s], 1.0, 0.0).astype(BF16)
+    for k in range(terms):
+        left[k] = left[k] * row_ok
+        right[:, k * cols:(k + 1) * cols] = right[:, k * cols:(k + 1) * cols] * col_ok
+
     @pl.when(after)
     def _():
         pl.semaphore_wait(told, 2 - core)
@@ -233,7 +239,7 @@
             prod[:, k * cols:(k + 1) * cols] = jnp.dot(
                 left[k], masked[shift[k] + 2], preferred_element_type=F32
             ).astype(BF16)
-        summed = lax.dot_general(prod[...], right[...], ROWS_BY_ROWS, preferred_element_type=F32) * mask[2].astype(F32)
+        summed = lax.dot_general(prod[...], right[...], ROWS_BY_ROWS, preferred_element_type=F32)
         total[v] = summed
         part[v] = summed.astype(BF16)
         if v == 0:

time: 30.9 us -> 30.9 us (level)
  no operation moved by 1% of the time
where the time goes in v5:
time: 30.9 us; the launch traced here: 30.8 us
  Pallas kernels  30.1 us (97%)
  local copies, waits for them, and re-layouts  0.62 us (2%)
    pallas_call x1, Pallas kernels, per_device(): pl.pallas_call(body, name='sigma', out_shape=jax.ShapeDtypeStruct((vecs,...  30.1 us
    unnamed x1, local copies, waits for them, and re-layouts  0.62 us

profile of v5, /device:TPU:7, one launch (start us, length us, event | category | flops | bytes accessed | tf_op | source)
XLA Modules:
  0.0 30.8 jit_solution(16330977826430064910)
XLA Ops:
  0.0 30.1 %sigma.1 = bf16[3,32,256]{2,1,0:T(8,128)(2,1)S(1)} custom-call(bf16[3,256,256]{2,1,0:T(8,128)(2,1)} %refs_0_.1, bf16[16,1,256,256]{3,2,1,0:T(8,128)(2,1)} %refs_1_.1, bf16[16,1,256,256]{3,2,1,0:T(8,128)(2,1)} %refs_2_.1, s32[16]{0:T(128)} %refs_3_.1, s32[64]{0:T(128)} %refs_4_.1, s32[64]{0:T(128)} %refs_5_.1), custom_call_target="tpu_custom_call" | custom-call | tf_op jit(solution)/shard_map/sigma/pallas_call | solution.py:285
  30.2 0.6 %copy.8 = bf16[3,32,256]{2,1,0:T(8,128)(2,1)} copy(bf16[3,32,256]{2,1,0:T(8,128)(2,1)S(1)} %sigma.1) | data formatting | bytes 98304
